TPU v7x, 256 devices: a whole 4x4x8 slice. The times are simulated.
256 devices in a mesh: blk: 4 (over x_hi, core), rows: 64 (over z, y, x_lo).
Axes of the slice: x: 4 (x_hi: 2, x_lo: 2; x = x_hi * 2 + x_lo), y: 4, z: 8, core: 2. Of those that a mesh axis runs over, the one named last changes fastest.
Arguments:
- volume: float32 [128, 1024, 1024], P('blk', 'rows'), may hold values from 0 to 1
- col_norm: float32 [128, 1024, 1024], P('blk', 'rows'), may hold values from 0.25 to 2
- measured: float32 [8, 1024, 1024], P(None, 'rows'), may hold values from -6 to 6
- row_norm: float32 [8, 1024, 1024], P(None, 'rows'), may hold values from 0.25 to 2
- tile_table: bfloat16 [64, 128, 128], replicated, may hold values from -0.09375 to 0.09375
- tile_index: int32 [32, 128, 64, 8], P(None, 'blk', 'rows'), may hold values from 0 to 63
- subset: int32 [8], replicated, may hold values from 0 to 31, as said below
- routes: int32 [16384, 1], P(('blk', 'rows')), may hold values from 0 to 63; in each aligned block of 64 rows (0 to 63, 64 to 127, ...) at most 2 rows name the same one
Outputs:
- updated_volume: float32 [128, 1024, 1024], P('blk', 'rows')
Inputs may be any that keep to these rules, and one draw needn't show every extreme that they name: `subset`: 8 distinct view numbers of the 32. `routes`: the 64 items of one device (view, then column block) name one detector row tile at most 2 times.
All inputs are finite; a program needn't handle non-finite values.
Results may differ from a plain program's by a relative error of at most 0.0035.
Values may be sent and summed in bfloat16 or wider, within the bound.
No kernel may reach another device: no remote copies, remote signals or barrier semaphores. Data moves between devices by JAX's collectives and lax.ppermute only.
A program may use at most 64 MiB of HBM per device.

v0:
```python
import jax
import jax.numpy as jnp
from jax import lax
from jax.sharding import PartitionSpec as P


def local(volume, col_norm, measured, row_norm, tile_table, tile_index, subset, routes):
    plane_count, tile_rows, width_cols = volume.shape
    view_count = measured.shape[0]
    table_count = tile_table.shape[0]
    block_cols = tile_table.shape[1]
    column_block_count = width_cols // block_cols
    item_count = view_count * column_block_count
    peer_count = lax.axis_size("rows")
    capacity = 2 * item_count // peer_count
    slot_count = peer_count * capacity
    tile_size = tile_rows * block_cols
    vol_blocks = volume.astype(jnp.bfloat16).reshape(
        plane_count, tile_rows, column_block_count, block_cols
    )
    chosen = jnp.take(tile_index[:, :, 0, :], subset, axis=0)
    table_wide = tile_table.astype(jnp.float32)
    table_ids = jnp.arange(table_count, dtype=jnp.int32)

    def forward(index_rows):
        picker = (index_rows[:, :, None] == table_ids[None, None, :]).astype(jnp.bfloat16)
        grouped = jnp.einsum(
            "zct,zrck->ctrk", picker, vol_blocks, preferred_element_type=jnp.float32
        )
        return jnp.einsum("ctrk,tke->cre", grouped, table_wide, precision=lax.Precision.HIGHEST)

    partial_value = lax.map(forward, chosen).astype(jnp.bfloat16).reshape(item_count, tile_size)
    dest_rows = routes[:, 0]
    hit_table = (dest_rows[:, None] == jnp.arange(peer_count, dtype=jnp.int32)[None, :]).astype(
        jnp.int32
    )
    rank_in = jnp.sum(jnp.cumsum(hit_table, axis=0) * hit_table, axis=1) - 1
    slot_of = dest_rows * capacity + rank_in
    placer = slot_of[None, :] == jnp.arange(slot_count, dtype=jnp.int32)[:, None]
    placer_half = placer.astype(jnp.bfloat16)
    send_tiles = jnp.dot(placer_half, partial_value, preferred_element_type=jnp.float32).astype(
        jnp.bfloat16
    )
    item_numbers = jnp.arange(item_count, dtype=jnp.int32)
    send_ids = jnp.sum(jnp.where(placer, item_numbers[None, :] + 1, 0), axis=1) - 1
    got_tiles, got_ids = (
        lax.all_to_all(
            send_tiles.reshape(peer_count, capacity * tile_size),
            "rows",
            split_axis=0,
            concat_axis=0,
            tiled=True,
        ),
        lax.all_to_all(
            send_ids.reshape(peer_count, capacity), "rows", split_axis=0, concat_axis=0, tiled=True
        ),
    )
    got_tiles = got_tiles.reshape(slot_count, tile_size)
    got_ids = got_ids.reshape(slot_count)
    taker_half = (item_numbers[:, None] == got_ids[None, :]).astype(jnp.bfloat16)
    local_proj = jnp.dot(taker_half, got_tiles, preferred_element_type=jnp.float32)
    measurement_items = (
        measured.reshape(view_count, tile_rows, column_block_count, block_cols)
        .transpose(0, 2, 1, 3)
        .reshape(item_count, tile_size)
    )
    normalizer_items = (
        row_norm.reshape(view_count, tile_rows, column_block_count, block_cols)
        .transpose(0, 2, 1, 3)
        .reshape(item_count, tile_size)
    )
    total_projection = lax.psum(local_proj, "blk")
    residual_error = (normalizer_items * (measurement_items - total_projection)).astype(
        jnp.bfloat16
    )
    back_send = jnp.dot(
        jnp.transpose(taker_half), residual_error, preferred_element_type=jnp.float32
    ).astype(jnp.bfloat16)
    returned = lax.all_to_all(
        back_send.reshape(peer_count, capacity * tile_size),
        "rows",
        split_axis=0,
        concat_axis=0,
        tiled=True,
    )
    returned = returned.reshape(slot_count, tile_size)
    item_resid = jnp.dot(
        jnp.transpose(placer_half), returned, preferred_element_type=jnp.float32
    ).astype(jnp.bfloat16)
    item_resid = item_resid.reshape(view_count, column_block_count, tile_rows, block_cols)

    def backward(running, inputs):
        index_rows, res_tile = inputs
        spread = jnp.einsum(
            "cre,tke->ctrk", res_tile, tile_table, preferred_element_type=jnp.float32
        )
        picker = (index_rows[:, :, None] == table_ids[None, None, :]).astype(jnp.float32)
        return (
            running + jnp.einsum("zct,ctrk->zrck", picker, spread, precision=lax.Precision.HIGHEST),
            None,
        )

    start = jnp.zeros((plane_count, tile_rows, column_block_count, block_cols), jnp.float32)
    gradient, _ = lax.scan(backward, start, (chosen, item_resid))
    gradient = gradient.reshape(plane_count, tile_rows, width_cols)
    return jnp.maximum(volume + col_norm * gradient, 0.0)


def solution(mesh):
    placed = (
        P("blk", "rows", None),
        P("blk", "rows", None),
        P(None, "rows", None),
        P(None, "rows", None),
        P(),
        P(None, "blk", "rows", None),
        P(),
        P(("blk", "rows"), None),
    )
    return jax.shard_map(
        local, mesh=mesh, in_specs=placed, out_specs=P("blk", "rows", None), check_vma=False
    )
```

profile of v0, /device:TPU:4, one launch (start us, length us, event | category | flops | bytes accessed | tf_op | source)
XLA Modules:
  0.0 316.7 jit_solution(14401755620140538130)
XLA Ops:
  9.8 12.7 %all-to-all-start = ((s32[64,1,2]{2,1,0:T(1,128)}), s32[64,1,2]{2,1,0:T(1,128)S(1)}, u32[]{:S(2)}, u32[]{:S(2)}) async-start(s32[64,1,2]{2,1,0:T(1,128)} %bitcast.1), calls=%async_computation | async-start | bytes 65536 | tf_op jit(solution)/shard_map/all_to_all | solution.py:54
  23.8 4.2 %convert_element_type.30 = f32[64,128,128]{2,1,0:T(8,128)} convert(bf16[64,128,128]{2,1,0:T(8,128)(2,1)} %param.16) | non-fusion elementwise | flops 1048576 | bytes 6291456 | tf_op jit(solution)/shard_map/convert_element_type | solution.py:22
  29.8 68.2 %while.22 = (s32[]{:T(128)}, bf16[8,8,16,128]{3,2,1,0:T(8,128)(2,1)S(1)}, s32[8,32,8]{1,2,0:T(8,128)S(1)}, bf16[32,16,8,128]{3,0,1,2:T(8,128)(2,1)S(1)}, f32[64,128,128]{2,1,0:T(8,128)}, /*index=5*/s32[]{:T(128)}) while((s32[]{:T(128)}, bf16[8,8,16,128]{3,2,1,0:T(8,128)(2,1)S(1)}, s32[8,32,8]{1,2,0:T(8,128)S(1)}, ...), condition=%wide.region_4.5_spmd.clone, body=%wide.region_3.4_spmd.clone.sunk | while | flops 1677737984 | bytes 30477416 | solution.py:32
  32.0 6.3 %fusion.59 = bf16[8,8,16,128]{3,2,1,0:T(8,128)(2,1)S(1)} fusion(bf16[8,8,16,128]{3,2,1,0:T(8,128)(2,1)S(1)} %get-tuple-element.229, s32[]{:T(128)} %get-tuple-element.228, f32[64,128,128]{2,1,0:T(8,128)S(1)} %copy-done.1, f32[8,64,16,128]{3,1,2,0:T(8,128)S(1)} %fusion.58), kind=kOutput, calls=%fused_computation.7.clone.1 | convolution fusion | flops 1610612736 | bytes 8454148 | tf_op jit(solution)/shard_map/while/body/eval_jaxpr/ctrk,tke->cre/dot_general | solution.py:30
  40.5 6.3 %fusion.59 = bf16[8,8,16,128]{3,2,1,0:T(8,128)(2,1)S(1)} fusion(bf16[8,8,16,128]{3,2,1,0:T(8,128)(2,1)S(1)} %get-tuple-element.229, s32[]{:T(128)} %get-tuple-element.228, f32[64,128,128]{2,1,0:T(8,128)S(1)} %copy-done.1, f32[8,64,16,128]{3,1,2,0:T(8,128)S(1)} %fusion.58), kind=kOutput, calls=%fused_computation.7.clone.1 | convolution fusion | flops 1610612736 | bytes 8454148 | tf_op jit(solution)/shard_map/while/body/eval_jaxpr/ctrk,tke->cre/dot_general | solution.py:30
  49.1 6.3 %fusion.59 = bf16[8,8,16,128]{3,2,1,0:T(8,128)(2,1)S(1)} fusion(bf16[8,8,16,128]{3,2,1,0:T(8,128)(2,1)S(1)} %get-tuple-element.229, s32[]{:T(128)} %get-tuple-element.228, f32[64,128,128]{2,1,0:T(8,128)S(1)} %copy-done.1, f32[8,64,16,128]{3,1,2,0:T(8,128)S(1)} %fusion.58), kind=kOutput, calls=%fused_computation.7.clone.1 | convolution fusion | flops 1610612736 | bytes 8454148 | tf_op jit(solution)/shard_map/while/body/eval_jaxpr/ctrk,tke->cre/dot_general | solution.py:30
  57.6 6.3 %fusion.59 = bf16[8,8,16,128]{3,2,1,0:T(8,128)(2,1)S(1)} fusion(bf16[8,8,16,128]{3,2,1,0:T(8,128)(2,1)S(1)} %get-tuple-element.229, s32[]{:T(128)} %get-tuple-element.228, f32[64,128,128]{2,1,0:T(8,128)S(1)} %copy-done.1, f32[8,64,16,128]{3,1,2,0:T(8,128)S(1)} %fusion.58), kind=kOutput, calls=%fused_computation.7.clone.1 | convolution fusion | flops 1610612736 | bytes 8454148 | tf_op jit(solution)/shard_map/while/body/eval_jaxpr/ctrk,tke->cre/dot_general | solution.py:30
  66.1 6.3 %fusion.59 = bf16[8,8,16,128]{3,2,1,0:T(8,128)(2,1)S(1)} fusion(bf16[8,8,16,128]{3,2,1,0:T(8,128)(2,1)S(1)} %get-tuple-element.229, s32[]{:T(128)} %get-tuple-element.228, f32[64,128,128]{2,1,0:T(8,128)S(1)} %copy-done.1, f32[8,64,16,128]{3,1,2,0:T(8,128)S(1)} %fusion.58), kind=kOutput, calls=%fused_computation.7.clone.1 | convolution fusion | flops 1610612736 | bytes 8454148 | tf_op jit(solution)/shard_map/while/body/eval_jaxpr/ctrk,tke->cre/dot_general | solution.py:30
  74.7 6.3 %fusion.59 = bf16[8,8,16,128]{3,2,1,0:T(8,128)(2,1)S(1)} fusion(bf16[8,8,16,128]{3,2,1,0:T(8,128)(2,1)S(1)} %get-tuple-element.229, s32[]{:T(128)} %get-tuple-element.228, f32[64,128,128]{2,1,0:T(8,128)S(1)} %copy-done.1, f32[8,64,16,128]{3,1,2,0:T(8,128)S(1)} %fusion.58), kind=kOutput, calls=%fused_computation.7.clone.1 | convolution fusion | flops 1610612736 | bytes 8454148 | tf_op jit(solution)/shard_map/while/body/eval_jaxpr/ctrk,tke->cre/dot_general | solution.py:30
  83.2 6.3 %fusion.59 = bf16[8,8,16,128]{3,2,1,0:T(8,128)(2,1)S(1)} fusion(bf16[8,8,16,128]{3,2,1,0:T(8,128)(2,1)S(1)} %get-tuple-element.229, s32[]{:T(128)} %get-tuple-element.228, f32[64,128,128]{2,1,0:T(8,128)S(1)} %copy-done.1, f32[8,64,16,128]{3,1,2,0:T(8,128)S(1)} %fusion.58), kind=kOutput, calls=%fused_computation.7.clone.1 | convolution fusion | flops 1610612736 | bytes 8454148 | tf_op jit(solution)/shard_map/while/body/eval_jaxpr/ctrk,tke->cre/dot_general | solution.py:30
  91.7 6.3 %fusion.59 = bf16[8,8,16,128]{3,2,1,0:T(8,128)(2,1)S(1)} fusion(bf16[8,8,16,128]{3,2,1,0:T(8,128)(2,1)S(1)} %get-tuple-element.229, s32[]{:T(128)} %get-tuple-element.228, f32[64,128,128]{2,1,0:T(8,128)S(1)} %copy-done.1, f32[8,64,16,128]{3,1,2,0:T(8,128)S(1)} %fusion.58), kind=kOutput, calls=%fused_computation.7.clone.1 | convolution fusion | flops 1610612736 | bytes 8454148 | tf_op jit(solution)/shard_map/while/body/eval_jaxpr/ctrk,tke->cre/dot_general | solution.py:30
  100.1 3.8 %reduce.6 = bf16[64,4096]{1,0:T(8,128)(2,1)S(1)} reduce(bf16[64,1,4096]{2,1,0:T(2,128)(2,1)S(1)} %all_to_all.21, bf16[]{:T(256)} %broadcast.67), dimensions={1}, to_apply=%all_to_all.21.reduce_sub_computation | reduce | bytes 1048578 | tf_op jit(solution)/shard_map/all_to_all | solution.py:47
  105.1 11.2 %all-to-all-start.1 = ((bf16[64,2,2048]{2,1,0:T(2,128)(2,1)}), bf16[64,2,2048]{2,1,0:T(2,128)(2,1)S(1)}, u32[]{:S(2)}, u32[]{:S(2)}) async-start(bf16[64,2,2048]{2,1,0:T(2,128)(2,1)} %reshape.119), calls=%async_computation.1 | async-start | bytes 1048576 | tf_op jit(solution)/shard_map/all_to_all | solution.py:47
  117.9 15.9 %all-to-all-done.1 = bf16[64,2,2048]{2,1,0:T(2,128)(2,1)S(1)} async-done(((bf16[64,2,2048]{2,1,0:T(2,128)(2,1)}), bf16[64,2,2048]{2,1,0:T(2,128)(2,1)S(1)}, u32[]{:S(2)}, u32[]{:S(2)}) %all-to-all-start.1) | async-done | bytes 524320 | tf_op jit(solution)/shard_map/all_to_all | solution.py:47
  134.4 3.1 reduce.1
  139.0 41.3 %all-reduce.2.cloned.1.call-done = f32[64,2048]{1,0:T(8,128)} async-done(((f32[64,2048]{1,0:T(8,128)}), f32[64,2048]{1,0:T(8,128)}) %all-reduce.2.cloned.1.call-update) | async-done | bytes 524304 | tf_op jit(solution)/shard_map/psum | solution.py:72
  182.5 3.8 %reduce.7 = bf16[64,4096]{1,0:T(8,128)(2,1)S(1)} reduce(bf16[64,1,4096]{2,1,0:T(2,128)(2,1)S(1)} %all_to_all.22, bf16[]{:T(256)} %broadcast.67), dimensions={1}, to_apply=%all_to_all.22.reduce_sub_computation | reduce | bytes 1048578 | tf_op jit(solution)/shard_map/all_to_all | solution.py:79
  187.6 11.9 %all-to-all-start.2 = ((bf16[64,2,2048]{2,1,0:T(2,128)(2,1)}), bf16[64,2,2048]{2,1,0:T(2,128)(2,1)S(1)}, u32[]{:S(2)}, u32[]{:S(2)}) async-start(bf16[64,2,2048]{2,1,0:T(2,128)(2,1)} %reshape.121), calls=%async_computation.2 | async-start | bytes 1048576 | tf_op jit(solution)/shard_map/all_to_all | solution.py:79
  199.5 18.1 %all-to-all-done.2 = bf16[64,2,2048]{2,1,0:T(2,128)(2,1)S(1)} async-done(((bf16[64,2,2048]{2,1,0:T(2,128)(2,1)}), bf16[64,2,2048]{2,1,0:T(2,128)(2,1)S(1)}, u32[]{:S(2)}, u32[]{:S(2)}) %all-to-all-start.2) | async-done | bytes 524320 | tf_op jit(solution)/shard_map/all_to_all | solution.py:79
  218.1 3.9 %reduce.2 = bf16[64,4096]{1,0:T(8,128)(2,1)} reduce(bf16[64,1,4096]{2,1,0:T(2,128)(2,1)S(1)} %reshape.122, bf16[]{:T(256)} %constant.58), dimensions={1}, to_apply=%all_to_all.20.reduce_sub_computation | reduce | bytes 1048578 | tf_op jit(solution)/shard_map/all_to_all | solution.py:79
  223.6 76.9 %while.23 = (s32[]{:T(128)}, f32[32,16,8,128]{3,0,1,2:T(8,128)}, bf16[8,8,16,128]{3,1,2,0:T(8,128)(2,1)S(1)}, bf16[64,128,128]{2,1,0:T(8,128)(2,1)S(1)}, s32[8,32,8]{1,2,0:T(8,128)S(1)}, /*index=5*/s32[]{:T(128)}, s32[]{:T(128)}) while((s32[]{:T(128)}, f32[32,16,8,128]{3,0,1,2:T(8,128)}, bf16[8,8,16,128]{3,1,2,0:T(8,128)(2,1)S(1)}, ...), condition=%wide.region_7.8_spmd.clone, body=%wide.region_6.7_spmd.clone.sunk | while | flops 672153600 | bytes 14781535 | solution.py:104
  223.6 2.6 convolution_bitcast_fusion.2
  226.2 6.4 %bitcast_add_fusion.2 = f32[32,16,8,128]{3,0,1,2:T(8,128)} fusion(f32[32,16,8,128]{3,0,1,2:T(8,128)} %get-tuple-element.248, f32[8,64,16,128]{3,2,1,0:T(8,128)} %convolution_bitcast_fusion.2, pred[]{:T(512)S(6)} %compare.3, s32[32,8]{0,1:T(8,128)S(1)} %dynamic-slice_bitcast_fusion.5), kind=kOutput, calls=%fused_computation.16.clone.1 | convolution fusion | flops 403718144 | bytes 8389633 | tf_op jit(solution)/shard_map/while/body/eval_jaxpr/zct,ctrk->zrck/dot_general | solution.py:99
  235.2 7.1 %bitcast_add_fusion.2 = f32[32,16,8,128]{3,0,1,2:T(8,128)} fusion(f32[32,16,8,128]{3,0,1,2:T(8,128)} %get-tuple-element.248, f32[8,64,16,128]{3,2,1,0:T(8,128)} %convolution_bitcast_fusion.2, pred[]{:T(512)S(6)} %compare.3, s32[32,8]{0,1:T(8,128)S(1)} %dynamic-slice_bitcast_fusion.5), kind=kOutput, calls=%fused_computation.16.clone.1 | convolution fusion | flops 403718144 | bytes 8389633 | tf_op jit(solution)/shard_map/while/body/eval_jaxpr/zct,ctrk->zrck/dot_general | solution.py:99
  244.9 7.1 %bitcast_add_fusion.2 = f32[32,16,8,128]{3,0,1,2:T(8,128)} fusion(f32[32,16,8,128]{3,0,1,2:T(8,128)} %get-tuple-element.248, f32[8,64,16,128]{3,2,1,0:T(8,128)} %convolution_bitcast_fusion.2, pred[]{:T(512)S(6)} %compare.3, s32[32,8]{0,1:T(8,128)S(1)} %dynamic-slice_bitcast_fusion.5), kind=kOutput, calls=%fused_computation.16.clone.1 | convolution fusion | flops 403718144 | bytes 8389633 | tf_op jit(solution)/shard_map/while/body/eval_jaxpr/zct,ctrk->zrck/dot_general | solution.py:99
  254.6 7.1 %bitcast_add_fusion.2 = f32[32,16,8,128]{3,0,1,2:T(8,128)} fusion(f32[32,16,8,128]{3,0,1,2:T(8,128)} %get-tuple-element.248, f32[8,64,16,128]{3,2,1,0:T(8,128)} %convolution_bitcast_fusion.2, pred[]{:T(512)S(6)} %compare.3, s32[32,8]{0,1:T(8,128)S(1)} %dynamic-slice_bitcast_fusion.5), kind=kOutput, calls=%fused_computation.16.clone.1 | convolution fusion | flops 403718144 | bytes 8389633 | tf_op jit(solution)/shard_map/while/body/eval_jaxpr/zct,ctrk->zrck/dot_general | solution.py:99
  264.3 7.1 %bitcast_add_fusion.2 = f32[32,16,8,128]{3,0,1,2:T(8,128)} fusion(f32[32,16,8,128]{3,0,1,2:T(8,128)} %get-tuple-element.248, f32[8,64,16,128]{3,2,1,0:T(8,128)} %convolution_bitcast_fusion.2, pred[]{:T(512)S(6)} %compare.3, s32[32,8]{0,1:T(8,128)S(1)} %dynamic-slice_bitcast_fusion.5), kind=kOutput, calls=%fused_computation.16.clone.1 | convolution fusion | flops 403718144 | bytes 8389633 | tf_op jit(solution)/shard_map/while/body/eval_jaxpr/zct,ctrk->zrck/dot_general | solution.py:99
  274.0 7.1 %bitcast_add_fusion.2 = f32[32,16,8,128]{3,0,1,2:T(8,128)} fusion(f32[32,16,8,128]{3,0,1,2:T(8,128)} %get-tuple-element.248, f32[8,64,16,128]{3,2,1,0:T(8,128)} %convolution_bitcast_fusion.2, pred[]{:T(512)S(6)} %compare.3, s32[32,8]{0,1:T(8,128)S(1)} %dynamic-slice_bitcast_fusion.5), kind=kOutput, calls=%fused_computation.16.clone.1 | convolution fusion | flops 403718144 | bytes 8389633 | tf_op jit(solution)/shard_map/while/body/eval_jaxpr/zct,ctrk->zrck/dot_general | solution.py:99
  283.7 7.1 %bitcast_add_fusion.2 = f32[32,16,8,128]{3,0,1,2:T(8,128)} fusion(f32[32,16,8,128]{3,0,1,2:T(8,128)} %get-tuple-element.248, f32[8,64,16,128]{3,2,1,0:T(8,128)} %convolution_bitcast_fusion.2, pred[]{:T(512)S(6)} %compare.3, s32[32,8]{0,1:T(8,128)S(1)} %dynamic-slice_bitcast_fusion.5), kind=kOutput, calls=%fused_computation.16.clone.1 | convolution fusion | flops 403718144 | bytes 8389633 | tf_op jit(solution)/shard_map/while/body/eval_jaxpr/zct,ctrk->zrck/dot_general | solution.py:99
  293.4 7.1 %bitcast_add_fusion.2 = f32[32,16,8,128]{3,0,1,2:T(8,128)} fusion(f32[32,16,8,128]{3,0,1,2:T(8,128)} %get-tuple-element.248, f32[8,64,16,128]{3,2,1,0:T(8,128)} %convolution_bitcast_fusion.2, pred[]{:T(512)S(6)} %compare.3, s32[32,8]{0,1:T(8,128)S(1)} %dynamic-slice_bitcast_fusion.5), kind=kOutput, calls=%fused_computation.16.clone.1 | convolution fusion | flops 403718144 | bytes 8389633 | tf_op jit(solution)/shard_map/while/body/eval_jaxpr/zct,ctrk->zrck/dot_general | solution.py:99
  300.4 2.8 copy.36
  304.7 5.1 %add_maximum_fusion = f32[32,16,1024]{2,1,0:T(8,128)} fusion(f32[32,16,1024]{2,1,0:T(8,128)} %param.12, f32[32,16,1024]{2,1,0:T(8,128)} %param.13, f32[32,16,1024]{2,1,0:T(8,128)} %reshape.92), kind=kLoop, calls=%fused_computation.27 | loop fusion | flops 1572864 | bytes 8388608 | tf_op jit(solution)/shard_map/max | solution.py:106
  (104 shorter events, 55.9 us)
Async XLA Ops:
  6.5 22.6 %copy-start = (s32[32,32,1,8]{1,3,2,0:T(8,128)S(1)}, s32[32,32,1,8]{1,3,2,0:T(8,128)}, u32[]{:S(2)}) copy-start(s32[32,32,1,8]{1,3,2,0:T(8,128)} %param.17) | copy-start | bytes 98308
  9.8 95.4 %all-to-all-start = ((s32[64,1,2]{2,1,0:T(1,128)}), s32[64,1,2]{2,1,0:T(1,128)S(1)}, u32[]{:S(2)}, u32[]{:S(2)}) async-start(s32[64,1,2]{2,1,0:T(1,128)} %bitcast.1), calls=%async_computation | async-start | bytes 65536 | tf_op jit(solution)/shard_map/all_to_all | solution.py:54
  23.8 4.2 %copy-start.3 = (f32[32,16,1024]{2,1,0:T(8,128)S(1)}, f32[32,16,1024]{2,1,0:T(8,128)}, u32[]{:S(2)}) copy-start(f32[32,16,1024]{2,1,0:T(8,128)} %param.12) | copy-start | bytes 6291460
  29.8 2.2 copy-start.1
  38.4 2.2 copy-start.1
  46.9 2.2 copy-start.1
  55.4 2.2 copy-start.1
  63.9 2.2 copy-start.1
  72.5 2.2 copy-start.1
  81.0 2.2 copy-start.1
  89.5 2.2 copy-start.1
  105.1 28.7 %all-to-all-start.1 = ((bf16[64,2,2048]{2,1,0:T(2,128)(2,1)}), bf16[64,2,2048]{2,1,0:T(2,128)(2,1)S(1)}, u32[]{:S(2)}, u32[]{:S(2)}) async-start(bf16[64,2,2048]{2,1,0:T(2,128)(2,1)} %reshape.119), calls=%async_computation.1 | async-start | bytes 1048576 | tf_op jit(solution)/shard_map/all_to_all | solution.py:47
  116.3 63.9 %all-reduce.2.cloned.1.call-start = ((), (), s32[]{:S(2)}) async-start(), calls=%async_computation.3 | async-start | bytes 1048576 | tf_op jit(solution)/shard_map/psum | solution.py:72
  134.4 4.4 %copy-start.4 = (f32[8,16,1024]{2,1,0:T(8,128)S(1)}, f32[8,16,1024]{2,1,0:T(8,128)}, u32[]{:S(2)}) copy-start(f32[8,16,1024]{2,1,0:T(8,128)} %param.14) | copy-start | bytes 1572868
  137.5 1.4 copy-start.5
  187.6 30.0 %all-to-all-start.2 = ((bf16[64,2,2048]{2,1,0:T(2,128)(2,1)}), bf16[64,2,2048]{2,1,0:T(2,128)(2,1)S(1)}, u32[]{:S(2)}, u32[]{:S(2)}) async-start(bf16[64,2,2048]{2,1,0:T(2,128)(2,1)} %reshape.121), calls=%async_computation.2 | async-start | bytes 1048576 | tf_op jit(solution)/shard_map/all_to_all | solution.py:79
  218.1 5.4 %copy-start.2 = (bf16[64,128,128]{2,1,0:T(8,128)(2,1)S(1)}, bf16[64,128,128]{2,1,0:T(8,128)(2,1)}, u32[]{:S(2)}) copy-start(bf16[64,128,128]{2,1,0:T(8,128)(2,1)} %param.16) | copy-start | bytes 6291460
Sparse Core Ops, SparseCore 0:
  138.9 41.3 all-reduce.1
where the time goes:
time: 318 us; the launch traced here: 317 us
  matrix products  137 us (43%)
  waiting for transfers between devices  75.3 us (24%)
  starting transfers between devices  35.9 us (11%)
  other arithmetic  28.8 us (9%)
  local copies, waits for them, and re-layouts  25.8 us (8%)
  between operations  13.7 us (4%)
    dot_general x8, matrix products, backward(): jnp.einsum('zct,ctrk->zrck', picker, spread, precision=lax.Precision.HIGH...  55.7 us
    dot_general x8, matrix products, forward(): jnp.einsum('ctrk,tke->cre', grouped, table_wide, precision=lax.Precision....  50.5 us
    psum x1, waiting for transfers between devices, local(): total_projection = lax.psum(local_proj, 'blk')  41.3 us
    dot_general x8, matrix products, backward(): jnp.einsum('cre,tke->ctrk', res_tile, tile_table, preferred_element_type=...  21.1 us
    all_to_all x1, waiting for transfers between devices, local(): lax.all_to_all(back_send.reshape(peer_count, capacity * tile_size), 'rows...  18.1 us
    all_to_all x1, waiting for transfers between devices, local(): lax.all_to_all(send_tiles.reshape(peer_count, capacity * tile_size), 'row...  15.9 us
    all_to_all x1, starting transfers between devices, local(): lax.all_to_all(send_ids.reshape(peer_count, capacity), 'rows', split_axis...  12.7 us
    all_to_all x1, starting transfers between devices, local(): lax.all_to_all(back_send.reshape(peer_count, capacity * tile_size), 'rows...  11.9 us
  transfers between devices with their start and end apart: 4, of which 3 were waited for; matrix products, arithmetic and copies ran while one was open for 23% of the time, Pallas kernels for 0%

commit v1 on v0

v1 whole, which is shorter than its diff:
```python
import jax
import jax.numpy as jnp
from jax import lax
from jax.experimental import pallas as pl
from jax.experimental.pallas import tpu as pltpu
from jax.sharding import PartitionSpec as P

HALF = jnp.bfloat16
WIDE = jnp.float32
VMEM = pl.BlockSpec(memory_space=pltpu.VMEM)
SMEM = pl.BlockSpec(memory_space=pltpu.SMEM)


def assign_slots(route_ref, count_ref, slot_ref):
    @pl.loop(0, count_ref.shape[0])
    def _(t):
        count_ref[t] = 0

    @pl.loop(0, slot_ref.shape[0])
    def _(i):
        t = route_ref[i]
        rank = count_ref[t]
        slot_ref[i] = 2 * t + rank
        count_ref[t] = rank + 1


def forward_kernel(
    index_ref, route_ref, volume_ref, table_ref, send_ref, slab, count_ref, slot_ref, number_ref
):
    planes, rows, width = volume_ref.shape
    cols = table_ref.shape[1]
    blocks = width // cols
    views = index_ref.shape[0] // (planes * blocks)
    items = views * blocks
    peers = send_ref.shape[0]
    assign_slots(route_ref, count_ref, slot_ref)

    @pl.loop(0, 2 * peers)
    def _(s):
        number_ref[s] = items

    @pl.loop(0, items)
    def _(i):
        number_ref[slot_ref[i]] = i

    lane = lax.broadcasted_iota(jnp.int32, (8, cols), 1)

    @pl.loop(0, peers)
    def _(t):
        send_ref[t, : 2 * rows, :] = jnp.zeros((2 * rows, cols), HALF)
        numbers = jnp.where(lane == 0, number_ref[2 * t], number_ref[2 * t + 1])
        send_ref[t, 2 * rows :, :] = numbers.astype(WIDE).astype(HALF)

    for c in range(blocks):
        for z in range(planes):
            slab[c, :, z * cols : (z + 1) * cols] = volume_ref[
                z, :, c * cols : (c + 1) * cols
            ].astype(HALF)

    def put(i, value):
        s = slot_ref[i]
        start = pl.multiple_of((s % 2) * rows, rows)
        send_ref[s // 2, pl.ds(start, rows), :] = value.astype(HALF)

    @pl.loop(0, blocks)
    def _(c):
        @pl.loop(0, views // 4)
        def _(quad):
            def tile(v, z):
                return table_ref[index_ref[(v * planes + z) * blocks + c]]

            sums = [jnp.zeros((rows, 2 * cols), WIDE)] * 2
            for z in range(0, planes, 2):
                for h in range(2):
                    v = 4 * quad + 2 * h
                    weights = jnp.concatenate(
                        [
                            jnp.concatenate([tile(v, z), tile(v + 1, z)], axis=1),
                            jnp.concatenate([tile(v, z + 1), tile(v + 1, z + 1)], axis=1),
                        ],
                        axis=0,
                    )
                    sums[h] = sums[h] + jnp.dot(
                        slab[c, :, z * cols : (z + 2) * cols],
                        weights,
                        preferred_element_type=WIDE,
                    )
            for h in range(2):
                v = 4 * quad + 2 * h
                put(v * blocks + c, sums[h][:, :cols])
                put((v + 1) * blocks + c, sums[h][:, cols:])


def collect_kernel(core_ref, number_ref, got_ref, keep_ref, give_ref, total):
    rows = total.shape[1]
    half = keep_ref.shape[0]
    total[...] = jnp.zeros_like(total)

    @pl.loop(0, got_ref.shape[0])
    def _(j):
        for s in range(2):
            i = number_ref[2 * j + s]
            total[i] += got_ref[j, s * rows : (s + 1) * rows, :].astype(WIDE)

    core = core_ref[0]
    keep_ref[...] = total[pl.ds(core * half, half)]
    give_ref[...] = total[pl.ds((1 - core) * half, half)]


def residual_kernel(core_ref, near_ref, far_ref, measured_ref, norm_ref, out_ref):
    half, rows, cols = near_ref.shape
    blocks = measured_ref.shape[2] // cols
    views = half // blocks
    first = core_ref[0] * views
    for v in range(views):
        for c in range(blocks):
            i = v * blocks + c
            at = (first + v, slice(None), slice(c * cols, (c + 1) * cols))
            projection = near_ref[i] + far_ref[i].astype(WIDE)
            out_ref[i] = (norm_ref[at] * (measured_ref[at] - projection)).astype(HALF)


def pack_kernel(core_ref, number_ref, own_ref, other_ref, back_ref, both):
    half, rows, _ = own_ref.shape
    core = core_ref[0]
    both[pl.ds(core * half, half)] = own_ref[...]
    both[pl.ds((1 - core) * half, half)] = other_ref[...]
    both[2 * half] = jnp.zeros(both.shape[1:], HALF)

    @pl.loop(0, back_ref.shape[0])
    def _(j):
        for s in range(2):
            back_ref[j, s * rows : (s + 1) * rows, :] = both[number_ref[2 * j + s]]


def transpose_kernel(table_ref, out_ref):
    @pl.loop(0, table_ref.shape[0])
    def _(t):
        out_ref[t] = table_ref[t].T


def backward_kernel(
    index_ref, route_ref, back_ref, volume_ref, norm_ref, table_ref, out_ref, spread, count_ref, slot_ref
):
    planes, rows, width = volume_ref.shape
    cols = table_ref.shape[1]
    blocks = width // cols
    views = index_ref.shape[0] // (planes * blocks)
    assign_slots(route_ref, count_ref, slot_ref)
    for v in range(views):
        for c in range(blocks):
            s = slot_ref[v * blocks + c]
            start = pl.multiple_of((s % 2) * rows, rows)
            spread[c, :, v * cols : (v + 1) * cols] = back_ref[s // 2, pl.ds(start, rows), :]

    @pl.loop(0, blocks)
    def _(c):
        here = pl.ds(pl.multiple_of(c * cols, cols), cols)

        def tile(v, z):
            return table_ref[index_ref[(v * planes + z) * blocks + c]]

        @pl.loop(0, planes // 4)
        def _(quad):
            for h in range(2):
                z = 4 * quad + 2 * h
                total = jnp.zeros((rows, 2 * cols), WIDE)
                for v in range(0, views, 2):
                    weights = jnp.concatenate(
                        [
                            jnp.concatenate([tile(v, z), tile(v, z + 1)], axis=1),
                            jnp.concatenate([tile(v + 1, z), tile(v + 1, z + 1)], axis=1),
                        ],
                        axis=0,
                    )
                    total = total + jnp.dot(
                        spread[c, :, v * cols : (v + 2) * cols],
                        weights,
                        preferred_element_type=WIDE,
                    )
                for q in range(2):
                    gradient = total[:, q * cols : (q + 1) * cols]
                    out_ref[z + q, :, here] = jnp.maximum(
                        volume_ref[z + q, :, here] + norm_ref[z + q, :, here] * gradient, 0.0
                    )


def local(volume, col_norm, measured, row_norm, tile_table, tile_index, subset, routes):
    planes, rows, width = volume.shape
    views = measured.shape[0]
    cols = tile_table.shape[1]
    blocks = width // cols
    items = views * blocks
    half = items // 2
    peers = lax.axis_size("rows")
    shape = jax.ShapeDtypeStruct
    counters = [pltpu.SMEM((peers,), jnp.int32), pltpu.SMEM((items,), jnp.int32)]

    chosen = jnp.take(tile_index[:, :, 0, :], subset, axis=0).reshape(-1)
    route = routes[:, 0]
    core = (lax.axis_index("blk") % 2).reshape(1)
    turned = pl.pallas_call(
        transpose_kernel,
        out_shape=shape(tile_table.shape, HALF),
        in_specs=[VMEM],
        out_specs=VMEM,
        name="turn_table",
    )(tile_table)

    send = pl.pallas_call(
        forward_kernel,
        out_shape=shape((peers, 2 * rows + 8, cols), HALF),
        in_specs=[SMEM, SMEM, VMEM, VMEM],
        out_specs=VMEM,
        scratch_shapes=[pltpu.VMEM((blocks, rows, planes * cols), HALF)]
        + counters
        + [pltpu.SMEM((2 * peers,), jnp.int32)],
        name="forward",
    )(chosen, route, volume, tile_table)
    got = lax.all_to_all(send, "rows", split_axis=0, concat_axis=0, tiled=True)
    number = got[:, 2 * rows, :2].astype(jnp.int32).reshape(2 * peers)
    keep, give = pl.pallas_call(
        collect_kernel,
        out_shape=[shape((half, rows, cols), WIDE)] * 2,
        in_specs=[SMEM, SMEM, VMEM],
        out_specs=[VMEM, VMEM],
        scratch_shapes=[pltpu.VMEM((items + 1, rows, cols), WIDE)],
        name="collect",
    )(core, number, got)

    swap_core = [(i, i ^ 1) for i in range(4)]
    swap_chip = [(i, i ^ 2) for i in range(4)]
    near = keep + lax.ppermute(give, "blk", swap_core)
    far = lax.ppermute(near.astype(HALF), "blk", swap_chip)
    own = pl.pallas_call(
        residual_kernel,
        out_shape=shape((half, rows, cols), HALF),
        in_specs=[SMEM, VMEM, VMEM, VMEM, VMEM],
        out_specs=VMEM,
        name="residual",
    )(core, near, far, measured, row_norm)
    other = lax.ppermute(own, "blk", swap_core)
    back = pl.pallas_call(
        pack_kernel,
        out_shape=shape((peers, 2 * rows, cols), HALF),
        in_specs=[SMEM, SMEM, VMEM, VMEM],
        out_specs=VMEM,
        scratch_shapes=[pltpu.VMEM((items + 1, rows, cols), HALF)],
        name="pack",
    )(core, number, own, other)
    back = lax.all_to_all(back, "rows", split_axis=0, concat_axis=0, tiled=True)
    return pl.pallas_call(
        backward_kernel,
        out_shape=shape(volume.shape, WIDE),
        in_specs=[SMEM, SMEM, VMEM, VMEM, VMEM, VMEM],
        out_specs=VMEM,
        scratch_shapes=[pltpu.VMEM((blocks, rows, views * cols), HALF)] + counters,
        name="backward",
    )(chosen, route, back, volume, col_norm, turned)


def solution(mesh):
    placed = (
        P("blk", "rows", None),
        P("blk", "rows", None),
        P(None, "rows", None),
        P(None, "rows", None),
        P(),
        P(None, "blk", "rows", None),
        P(),
        P(("blk", "rows"), None),
    )
    return jax.shard_map(
        local, mesh=mesh, in_specs=placed, out_specs=P("blk", "rows", None), check_vma=False
    )
```

time: 318 us -> 121 us (0.38)
  matrix products: 137 us -> 0 us
  Pallas kernels: 0 us -> 53.3 us
  waiting for transfers between devices: 75.3 us -> 40.7 us
  other arithmetic: 28.8 us -> 3.23 us
  local copies, waits for them, and re-layouts: 25.8 us -> 4.19 us
  starting transfers between devices: 35.9 us -> 19.2 us
  between operations: 13.7 us -> 0.06 us
    dot_general x36 -> x0, matrix products: 137 us -> none  [the longest x8 55.7 us: backward(): jnp.einsum('zct,ctrk->zrck', picker, spread, precision=lax.Precision.HIGH...]
    pallas_call x0 -> x6, Pallas kernels: none -> 53.3 us  [the longest x1 22.2 us: local(): pl.pallas_call(backward_kernel, out_shape=shape(volume.shape, WIDE), in_s...]
    psum x1 -> x0, waiting for transfers between devices: 41.3 us -> none  [local(): total_projection = lax.psum(local_proj, 'blk')]
    all_to_all x3 -> x2, starting transfers between devices: 35.9 us -> 18.4 us  [the longest x1 12.7 us: local(): got = lax.all_to_all(send, 'rows', split_axis=0, concat_axis=0, tiled=True)]
    all_to_all x5 -> x0, other arithmetic: 15.5 us -> none  [the longest x2 7.78 us: local(): lax.all_to_all(back_send.reshape(peer_count, capacity * tile_size), 'rows...]
    while x17 -> x0, local copies, waits for them, and re-layouts: 13.7 us -> none
    ppermute x0 -> x3, waiting for transfers between devices: none -> 9.54 us  [the longest x1 6.24 us: local(): far = lax.ppermute(near.astype(HALF), 'blk', swap_chip)]
    max x1 -> x0, other arithmetic: 5.08 us -> none  [local(): return jnp.maximum(volume + col_norm * gradient, 0.0)]
  transfers between devices with their start and end apart: 4 -> 5, of which waited for: 3 -> 5; matrix products, arithmetic and copies ran while one was open for 23% -> 0% of each run, Pallas kernels for 0% -> 6%
where the time goes in v1:
time: 121 us
  Pallas kernels  53.3 us (44%)
  waiting for transfers between devices  40.7 us (34%)
  starting transfers between devices  19.2 us (16%)
  local copies, waits for them, and re-layouts  4.19 us (3%)
  other arithmetic  3.23 us (3%)
    pallas_call x1, Pallas kernels, local(): pl.pallas_call(backward_kernel, out_shape=shape(volume.shape, WIDE), in_s...  22.2 us
    all_to_all x1, waiting for transfers between devices, local(): got = lax.all_to_all(send, 'rows', split_axis=0, concat_axis=0, tiled=True)  20.7 us
    pallas_call x1, Pallas kernels, local(): pl.pallas_call(forward_kernel, out_shape=shape((peers, 2 * rows + 8, cols...  16.7 us
    all_to_all x1, starting transfers between devices, local(): got = lax.all_to_all(send, 'rows', split_axis=0, concat_axis=0, tiled=True)  12.7 us
    all_to_all x1, waiting for transfers between devices, local(): back = lax.all_to_all(back, 'rows', split_axis=0, concat_axis=0, tiled=True)  10.5 us
    pallas_call x1, Pallas kernels, local(): pl.pallas_call(transpose_kernel, out_shape=shape(tile_table.shape, HALF),...  7.44 us
    ppermute x1, waiting for transfers between devices, local(): far = lax.ppermute(near.astype(HALF), 'blk', swap_chip)  6.24 us
    all_to_all x1, starting transfers between devices, local(): back = lax.all_to_all(back, 'rows', split_axis=0, concat_axis=0, tiled=True)  5.63 us
  transfers between devices with their start and end apart: 5, of which 5 were waited for; matrix products, arithmetic and copies ran while one was open for 0% of the time, Pallas kernels for 6%

profile of v1, /device:TPU:4, one launch (start us, length us, event | category | flops | bytes accessed | tf_op | source)
XLA Modules:
  0.0 120.7 jit_solution(7496132546344962225)
XLA Ops:
  0.0 0.0 copy-start
  0.0 0.7 compare_and_fusion
  0.7 0.7 compare_select_fusion
  1.4 0.0 copy-done
  1.4 0.6 gather_fusion
  1.9 0.1 broadcast_select_fusion
  2.0 0.1 copy.9
  2.1 0.7 select_n.22.index_ref
  2.8 16.7 %forward.1 = bf16[64,40,128]{2,1,0:T(8,128)(2,1)} custom-call(s32[2048]{0:T(1024)} %select_n.22.index_ref, s32[64]{0:T(128)} %bitcast.4, f32[32,16,1024]{2,1,0:T(8,128)} %volume_ref.3, bf16[64,128,128]{2,1,0:T(8,128)(2,1)} %table_ref.3), custom_call_target="tpu_custom_call" | custom-call | tf_op jit(solution)/shard_map/forward/pallas_call | solution.py:210
  19.5 12.7 %all-to-all-start = ((bf16[64,40,128]{2,1,0:T(8,128)(2,1)}), bf16[64,40,128]{2,1,0:T(8,128)(2,1)S(1)}, u32[]{:S(2)}, u32[]{:S(2)}) async-start(bf16[64,40,128]{2,1,0:T(8,128)(2,1)} %forward.1), calls=%async_computation | async-start | bytes 1310720 | tf_op jit(solution)/shard_map/all_to_all | solution.py:220
  32.2 20.7 %all-to-all-done.got_ref = bf16[64,40,128]{2,1,0:T(8,128)(2,1)S(1)} async-done(((bf16[64,40,128]{2,1,0:T(8,128)(2,1)}), bf16[64,40,128]{2,1,0:T(8,128)(2,1)S(1)}, u32[]{:S(2)}, u32[]{:S(2)}) %all-to-all-start) | async-done | bytes 655392 | tf_op jit(solution)/shard_map/all_to_all | solution.py:220
  52.9 0.0 copy-start.1
  52.9 0.1 fusion
  53.0 0.7 reshape.18.number_ref
  53.7 0.1 copy-done.1
  53.7 2.7 %collect.1 = (f32[32,16,128]{2,1,0:T(8,128)}, f32[32,16,128]{2,1,0:T(8,128)}) custom-call(s32[1]{0:T(128)} %bitcast.2.core_ref, s32[128]{0:T(128)} %reshape.18.number_ref, bf16[64,40,128]{2,1,0:T(8,128)(2,1)} %copy-done.1), custom_call_target="tpu_custom_call" | custom-call | tf_op jit(solution)/shard_map/collect/pallas_call | solution.py:222
  56.4 0.0 collective-permute-start
  56.4 1.7 %collective-permute-done = f32[32,16,128]{2,1,0:T(8,128)S(1)} collective-permute-done((f32[32,16,128]{2,1,0:T(8,128)}, f32[32,16,128]{2,1,0:T(8,128)S(1)}, u32[]{:S(2)}, u32[]{:S(2)}) %collective-permute-start) | collective-permute-done | bytes 262176 | tf_op jit(solution)/shard_map/ppermute | solution.py:233
  58.2 1.7 %fusion.1 = (bf16[32,16,128]{2,1,0:T(8,128)(2,1)S(1)}, f32[32,16,128]{2,1,0:T(8,128)}) fusion(f32[32,16,128]{2,1,0:T(8,128)} %get-tuple-element.7, f32[32,16,128]{2,1,0:T(8,128)S(1)} %collective-permute-done), kind=kLoop, calls=%fused_computation.7 | loop fusion | flops 131072 | bytes 917504 | tf_op jit(solution)/shard_map/convert_element_type | solution.py:234
  59.9 0.8 collective-permute-start.1
  60.7 6.2 %collective-permute-done.1.far_ref = bf16[32,16,128]{2,1,0:T(8,128)(2,1)S(1)} collective-permute-done((bf16[32,16,128]{2,1,0:T(8,128)(2,1)S(1)}, bf16[32,16,128]{2,1,0:T(8,128)(2,1)S(1)}, u32[]{:S(2)}, u32[]{:S(2)}) %collective-permute-start.1) | collective-permute-done | bytes 131104 | tf_op jit(solution)/shard_map/ppermute | solution.py:234
  66.9 0.7 copy-done.3
  67.6 2.0 %residual.1.own_ref = bf16[32,16,128]{2,1,0:T(8,128)(2,1)} custom-call(s32[1]{0:T(128)} %bitcast.2.core_ref, f32[32,16,128]{2,1,0:T(8,128)} %get-tuple-element.10.near_ref, bf16[32,16,128]{2,1,0:T(8,128)(2,1)} %copy-done.3, f32[8,16,1024]{2,1,0:T(8,128)} %measured_ref.1, f32[8,16,1024]{2,1,0:T(8,128)} %norm_ref.2), custom_call_target="tpu_custom_call" | custom-call | tf_op jit(solution)/shard_map/residual/pallas_call | solution.py:235
  69.6 0.0 collective-permute-start.2
  69.6 1.6 %collective-permute-done.2.other_ref = bf16[32,16,128]{2,1,0:T(8,128)(2,1)S(1)} collective-permute-done((bf16[32,16,128]{2,1,0:T(8,128)(2,1)}, bf16[32,16,128]{2,1,0:T(8,128)(2,1)S(1)}, u32[]{:S(2)}, u32[]{:S(2)}) %collective-permute-start.2) | collective-permute-done | bytes 131104 | tf_op jit(solution)/shard_map/ppermute | solution.py:242
  71.2 0.7 copy-done.4
  71.8 2.3 %pack.1 = bf16[64,32,128]{2,1,0:T(8,128)(2,1)} custom-call(s32[1]{0:T(128)} %bitcast.2.core_ref, s32[128]{0:T(128)} %reshape.18.number_ref, bf16[32,16,128]{2,1,0:T(8,128)(2,1)} %residual.1.own_ref, bf16[32,16,128]{2,1,0:T(8,128)(2,1)} %copy-done.4), custom_call_target="tpu_custom_call" | custom-call | tf_op jit(solution)/shard_map/pack/pallas_call | solution.py:243
  74.1 5.6 %all-to-all-start.1 = ((bf16[64,32,128]{2,1,0:T(8,128)(2,1)}), bf16[64,32,128]{2,1,0:T(8,128)(2,1)S(1)}, u32[]{:S(2)}, u32[]{:S(2)}) async-start(bf16[64,32,128]{2,1,0:T(8,128)(2,1)} %pack.1), calls=%async_computation.1 | async-start | bytes 1048576 | tf_op jit(solution)/shard_map/all_to_all | solution.py:251
  79.7 7.4 %turn_table.1.table_ref = bf16[64,128,128]{2,1,0:T(8,128)(2,1)} custom-call(bf16[64,128,128]{2,1,0:T(8,128)(2,1)} %table_ref.3), custom_call_target="tpu_custom_call" | custom-call | tf_op jit(solution)/shard_map/turn_table/pallas_call | solution.py:202
  87.2 10.5 %all-to-all-done.1.back_ref = bf16[64,32,128]{2,1,0:T(8,128)(2,1)S(1)} async-done(((bf16[64,32,128]{2,1,0:T(8,128)(2,1)}), bf16[64,32,128]{2,1,0:T(8,128)(2,1)S(1)}, u32[]{:S(2)}, u32[]{:S(2)}) %all-to-all-start.1) | async-done | bytes 524320 | tf_op jit(solution)/shard_map/all_to_all | solution.py:251
  97.7 0.8 copy-done.2
  98.5 22.2 %backward.1 = f32[32,16,1024]{2,1,0:T(8,128)} custom-call(s32[2048]{0:T(1024)} %select_n.22.index_ref, s32[64]{0:T(128)} %bitcast.5, bf16[64,32,128]{2,1,0:T(8,128)(2,1)} %copy-done.2, f32[32,16,1024]{2,1,0:T(8,128)} %volume_ref.3, f32[32,16,1024]{2,1,0:T(8,128)} %norm_ref.3, bf16[64,128,128]{2,1,0:T(8,128)(2,1)} %turn_table.1.table_ref), custom_call_target="tpu_custom_call" | custom-call | tf_op jit(solution)/shard_map/backward/pallas_call | solution.py:252
  (4 shorter events, 0.0 us)
Async XLA Ops:
  0.0 1.4 %copy-start = (s32[32,32,1,8]{1,3,2,0:T(8,128)S(1)}, s32[32,32,1,8]{1,3,2,0:T(8,128)}, u32[]{:S(2)}) copy-start(s32[32,32,1,8]{1,3,2,0:T(8,128)} %param.13) | copy-start | bytes 98308
  19.5 33.4 %all-to-all-start = ((bf16[64,40,128]{2,1,0:T(8,128)(2,1)}), bf16[64,40,128]{2,1,0:T(8,128)(2,1)S(1)}, u32[]{:S(2)}, u32[]{:S(2)}) async-start(bf16[64,40,128]{2,1,0:T(8,128)(2,1)} %forward.1), calls=%async_computation | async-start | bytes 1310720 | tf_op jit(solution)/shard_map/all_to_all | solution.py:220
  52.9 0.8 copy-start.1
  56.4 1.7 %collective-permute-start = (f32[32,16,128]{2,1,0:T(8,128)}, f32[32,16,128]{2,1,0:T(8,128)S(1)}, u32[]{:S(2)}, u32[]{:S(2)}) collective-permute-start(f32[32,16,128]{2,1,0:T(8,128)} %get-tuple-element.8), channel_id=1, source_target_pairs={{0,64},{64,0},{128,192},{192,128},{1,65},{65,1},{129,193},{193,129... | collective-permute-start | bytes 786440 | tf_op jit(solution)/shard_map/ppermute | solution.py:233
  59.9 7.0 %collective-permute-start.1 = (bf16[32,16,128]{2,1,0:T(8,128)(2,1)S(1)}, bf16[32,16,128]{2,1,0:T(8,128)(2,1)S(1)}, u32[]{:S(2)}, u32[]{:S(2)}) collective-permute-start(bf16[32,16,128]{2,1,0:T(8,128)(2,1)S(1)} %get-tuple-element.9), channel_id=1, source_target_pairs={{0,128},{64,192},{128,0},{192,64},{1,129},{65,193},{129,1},{193,65... | collective-permute-start | bytes 393224 | tf_op jit(solution)/shard_map/ppermute | solution.py:234
  66.9 0.7 copy-start.3
  69.6 1.6 %collective-permute-start.2 = (bf16[32,16,128]{2,1,0:T(8,128)(2,1)}, bf16[32,16,128]{2,1,0:T(8,128)(2,1)S(1)}, u32[]{:S(2)}, u32[]{:S(2)}) collective-permute-start(bf16[32,16,128]{2,1,0:T(8,128)(2,1)} %residual.1.own_ref), channel_id=1, source_target_pairs={{0,64},{64,0},{128,192},{192,128},{1,65},{65,1},{129,193},{193,129... | collective-permute-start | bytes 393224 | tf_op jit(solution)/shard_map/ppermute | solution.py:242
  71.2 0.7 copy-start.4
  74.1 23.6 %all-to-all-start.1 = ((bf16[64,32,128]{2,1,0:T(8,128)(2,1)}), bf16[64,32,128]{2,1,0:T(8,128)(2,1)S(1)}, u32[]{:S(2)}, u32[]{:S(2)}) async-start(bf16[64,32,128]{2,1,0:T(8,128)(2,1)} %pack.1), calls=%async_computation.1 | async-start | bytes 1048576 | tf_op jit(solution)/shard_map/all_to_all | solution.py:251
  97.7 0.8 copy-start.2
